TPU v7x, 32 devices: a whole 2x2x4 slice. The times are simulated.
32 devices in a mesh: ia: 4 (over z), ja: 4 (over y, x), ka: 2 (over core).
Axes of the slice: x: 2, y: 2, z: 4, core: 2. Of those that a mesh axis runs over, the one named last changes fastest.
Arguments:
- tensor: float32 [1024, 1024, 512], P('ia', 'ja', 'ka'), may hold values from -6 to 6
- factor_first: float32 [1024, 32], P(('ia', 'ja', 'ka')), may hold values from -0.75 to 0.75
- factor_second: float32 [1024, 32], P(('ja', 'ia', 'ka')), may hold values from -0.375 to 0.375
- factor_third: float32 [512, 32], P(('ka', 'ia', 'ja')), may hold values from -0.375 to 0.375
Outputs:
- gradient: float32 [1024, 32], P(('ia', 'ja', 'ka'))
All inputs are finite; a program needn't handle non-finite values.
Results may differ from a plain program's by a relative error of at most 0.000082.
Values sent between devices are 32-bit elements; how exact they have to be, the bound alone decides.
A program may use at most 128 MiB of HBM per device.

v0:
```python
import jax
import jax.numpy as jnp
from jax import lax
from jax.sharding import PartitionSpec as P


def on_device(tensor, factor_first, factor_second, factor_third):
    third_block = lax.all_gather(factor_third, ("ia", "ja"), axis=0, tiled=True)
    second_block = lax.all_gather(factor_second, ("ia", "ka"), axis=0, tiled=True)
    partial_value = jnp.einsum("ijk,kr->ijr", tensor, third_block, precision=lax.Precision.HIGHEST)
    term = jnp.einsum("ijr,jr->ir", partial_value, second_block, precision=lax.Precision.HIGHEST)
    local_second = jnp.dot(factor_second.T, factor_second, precision=lax.Precision.HIGHEST)
    local_third = jnp.dot(factor_third.T, factor_third, precision=lax.Precision.HIGHEST)
    gram_second, gram_third = lax.psum((local_second, local_third), ("ia", "ja", "ka"))
    product = lax.psum_scatter(term, ("ja", "ka"), scatter_dimension=0, tiled=True)
    return (
        jnp.dot(factor_first, gram_second * gram_third, precision=lax.Precision.HIGHEST) - product
    )


def solution(mesh):
    return jax.shard_map(
        on_device,
        mesh=mesh,
        in_specs=(
            P("ia", "ja", "ka"),
            P(("ia", "ja", "ka"), None),
            P(("ja", "ia", "ka"), None),
            P(("ka", "ia", "ja"), None),
        ),
        out_specs=P(("ia", "ja", "ka"), None),
        check_vma=False,
    )
```

profile of v0, /device:TPU:1, one launch (start us, length us, event | category | flops | bytes accessed | tf_op | source)
XLA Modules:
  0.0 199.4 jit_solution(17685033110799472953)
XLA Ops:
  6.5 0.0 copy-start
  6.5 0.0 reduce-scatter.4.cloned.1.call-start
  6.5 15.9 %all_gather.7 = f32[256,32]{1,0:T(8,128)S(1)} all-gather(f32[32,32]{1,0:T(8,128)} %param.6), channel_id=1, replica_groups=mesh['ia'=4,'ja'=4,'ka'=2] {'ia','ka'}, dimensions={0}, use_global_device_ids=true | all-gather | bytes 36864 | tf_op jit(solution)/shard_map/all_gather | solution.py:9
  22.5 0.1 copy.9
  22.5 34.6 %all_gather.6 = f32[256,32]{1,0:T(8,128)S(1)} all-gather(f32[16,32]{1,0:T(8,128)} %param.7), channel_id=1, replica_groups=mesh['ia'=4,'ja'=4,'ka'=2] {'ia','ja'}, dimensions={0}, use_global_device_ids=true | all-gather | bytes 34816 | tf_op jit(solution)/shard_map/all_gather | solution.py:8
  57.2 74.8 %fusion.3 = f32[256,256,32]{1,2,0:T(8,128)} fusion(f32[256,256,256]{2,1,0:T(8,128)} %param.4, f32[256,32]{1,0:T(8,128)S(1)} %all_gather.6), kind=kOutput, calls=%fused_computation.4 | convolution fusion | flops 6442450944 | bytes 75530240 | tf_op jit(solution)/shard_map/ijk,kr->ijr/dot_general | solution.py:10
  131.9 0.0 copy-start.1
  131.9 0.0 copy-start.2
  131.9 14.8 %fusion = f32[32,1,256]{2,1,0:T(1,128)S(1)} fusion(f32[256,32,1]{0,2,1:T(1,128)S(1)} %copy.9, f32[256,256,32]{1,2,0:T(8,128)} %fusion.3), kind=kOutput, calls=%fused_computation | convolution fusion | flops 25165824 | bytes 8454144 | tf_op jit(solution)/shard_map/ijr,jr->ir/dot_general | solution.py:11
  146.7 0.8 copy.13
  147.4 0.0 reduce-scatter.4.cloned.1.call-update
  147.5 0.0 copy-done.1
  147.5 0.2 fusion.6
  147.7 0.0 copy-done.2
  147.7 0.2 fusion.7
  147.9 42.9 %all-reduce = (f32[32,32]{1,0:T(8,128)S(1)}, f32[32,32]{1,0:T(8,128)S(1)}) all-reduce(f32[32,32]{1,0:T(8,128)S(1)} %fusion.6, f32[32,32]{1,0:T(8,128)S(1)} %fusion.7), channel_id=1, replica_groups=mesh['ia'=4,'ja'=4,'ka'=2] {'ia','ja','ka'}, use_global_device_ids=true, to_apply=%region_0.0 | all-reduce | flops 2048 | bytes 16384 | tf_op jit(solution)/shard_map/psum | solution.py:14
  190.8 0.0 reduce-scatter.4.cloned.1.call-done
  190.8 0.8 copy.12
  191.6 0.0 copy-done
  191.6 0.2 fusion.2
  191.8 0.7 copy.7
Async XLA Ops:
  6.5 185.1 %copy-start = (f32[32,32]{1,0:T(8,128)S(1)}, f32[32,32]{1,0:T(8,128)}, u32[]{:S(2)}) copy-start(f32[32,32]{1,0:T(8,128)} %param.5) | copy-start | bytes 12292
  6.5 184.3 %reduce-scatter.4.cloned.1.call-start = ((), (), s32[]{:S(2)}) async-start(), calls=%async_computation.1 | async-start | bytes 147456
  131.9 15.6 %copy-start.1 = (f32[32,32]{1,0:T(8,128)S(1)}, f32[32,32]{1,0:T(8,128)}, u32[]{:S(2)}) copy-start(f32[32,32]{1,0:T(8,128)} %param.6) | copy-start | bytes 12292
  131.9 15.8 %copy-start.2 = (f32[16,32]{1,0:T(8,128)S(1)}, f32[16,32]{1,0:T(8,128)}, u32[]{:S(2)}) copy-start(f32[16,32]{1,0:T(8,128)} %param.7) | copy-start | bytes 6148
Sparse Core Ops, SparseCore 0:
  147.6 35.2 reduce-scatter.3
where the time goes:
time: 202 us; the launch traced here: 199 us
  blocking collectives  93.4 us (46%)
  matrix products  90.2 us (45%)
  between operations  13.5 us (7%)
  local copies, waits for them, and re-layouts  2.32 us (1%)
    dot_general x1, matrix products, on_device(): jnp.einsum('ijk,kr->ijr', tensor, third_block, precision=lax.Precision.HI...  74.8 us
    psum x1, blocking collectives, on_device(): lax.psum((local_second, local_third), ('ia', 'ja', 'ka'))  42.9 us
    all_gather x1, blocking collectives, on_device(): third_block = lax.all_gather(factor_third, ('ia', 'ja'), axis=0, tiled=True)  34.6 us
    all_gather x1, blocking collectives, on_device(): lax.all_gather(factor_second, ('ia', 'ka'), axis=0, tiled=True)  15.9 us
    dot_general x1, matrix products, on_device(): jnp.einsum('ijr,jr->ir', partial_value, second_block, precision=lax.Preci...  14.8 us
  transfers between devices with their start and end apart: 1, of which 0 were waited for; matrix products, arithmetic and copies ran while one was open for 0% of the time, Pallas kernels for 0%

commit v1 on v0

v1 whole, which is shorter than its diff:
```python
import functools

import jax
import jax.numpy as jnp
from jax import lax
from jax.experimental import pallas as pl
from jax.experimental.pallas import tpu as pltpu
from jax.sharding import PartitionSpec as P

MESH = pl.DeviceIdType.MESH
HIGHEST = lax.Precision.HIGHEST
TOGETHER = 2
CHUNK_ROWS = 8
BUFFERS = 20
EARLY = 8


def split(x):
    high = x.astype(jnp.bfloat16)
    low = (x - high.astype(jnp.float32)).astype(jnp.bfloat16)
    return high, low


def kernel(
    na, nj, nk, chunk_rows, buffers,
    x_hbm, first_ref, second_ref, third_ref, out_ref,
    x_buf, x_sem,
    third_all, third_send, third_recv,
    second_all, second_send, second_recv,
    third_flat, second_flat, weights, scale,
    gram3, gram3_send, gram3_recv,
    gram2, gram2_send, gram2_recv,
    part, terms_out, terms_in, term_send, term_recv,
):
    ia, ja, ka = lax.axis_index("ia"), lax.axis_index("ja"), lax.axis_index("ka")
    n_owner = nj * nk
    own = ja * nk + ka
    rows = out_ref.shape[0]
    rank = out_ref.shape[1]
    per_owner = rows // chunk_rows
    chunks = n_owner * per_owner

    def owner_at(turn):
        return lax.rem(own + 1 + turn, n_owner)

    def x_copy(c):
        start = owner_at(c // per_owner) * rows + lax.rem(c, per_owner) * chunk_rows
        slot = lax.rem(c, buffers)
        return pltpu.make_async_copy(
            x_hbm.at[pl.ds(start, chunk_rows)], x_buf.at[slot], x_sem.at[slot]
        )

    def start_x(c, carry):
        x_copy(c).start()
        return carry

    early = min(EARLY, buffers)
    lax.fori_loop(0, early, start_x, 0)

    def third_peer(d):
        at = lax.rem(ia * nj + ja + d, na * nj)
        return at // nj, lax.rem(at, nj)

    def second_peer(d):
        at = lax.rem(ia * nk + ka + d, na * nk)
        return at // nk, lax.rem(at, nk)

    barrier = pltpu.get_barrier_semaphore()

    def greet(device):
        pl.semaphore_signal(barrier, inc=1, device_id=device, device_id_type=MESH)

    def greet_third(d, carry):
        pa, pj = third_peer(d)
        greet((pa, pj, ka))
        return carry

    lax.fori_loop(1, na * nj, greet_third, 0)
    for dk in range(1, nk):
        pk = lax.rem(ka + dk, nk)
        for da in range(na):
            greet((lax.rem(ia + da, na), ja, pk))
        for dj in range(1, nj):
            greet((ia, lax.rem(ja + dj, nj), pk))
    pl.semaphore_wait(barrier, na * nj - 1 + (nk - 1) * (na + nj - 1))

    third_at = ia * nj + ja
    second_at = ia * nk + ka

    def third_copy(d):
        pa, pj = third_peer(d)
        return pltpu.make_async_remote_copy(
            src_ref=third_ref, dst_ref=third_all.at[third_at],
            send_sem=third_send.at[d], recv_sem=third_recv.at[third_at],
            device_id=(pa, pj, ka), device_id_type=MESH,
        )

    def second_copy(d):
        pa, pk = second_peer(d)
        return pltpu.make_async_remote_copy(
            src_ref=second_ref, dst_ref=second_all.at[second_at],
            send_sem=second_send.at[d], recv_sem=second_recv.at[second_at],
            device_id=(pa, ja, pk), device_id_type=MESH,
        )

    def start_third(d, carry):
        third_copy(d).start()
        return carry

    def start_second(d, carry):
        second_copy(d).start()
        return carry

    lax.fori_loop(1, na * nj, start_third, 0)
    lax.fori_loop(1, na * nk, start_second, 0)
    lax.fori_loop(early, buffers, start_x, 0)
    third_all[third_at] = third_ref[...]
    second_all[second_at] = second_ref[...]

    def recv_third(d, carry):
        pa, pj = third_peer(d)
        at = pa * nj + pj
        pltpu.make_async_remote_copy(
            src_ref=third_ref, dst_ref=third_all.at[at],
            send_sem=third_send.at[d], recv_sem=third_recv.at[at],
            device_id=(pa, pj, ka), device_id_type=MESH,
        ).wait_recv()
        return carry

    def recv_second(d, carry):
        pa, pk = second_peer(d)
        at = pa * nk + pk
        pltpu.make_async_remote_copy(
            src_ref=second_ref, dst_ref=second_all.at[at],
            send_sem=second_send.at[d], recv_sem=second_recv.at[at],
            device_id=(pa, ja, pk), device_id_type=MESH,
        ).wait_recv()
        return carry

    lax.fori_loop(1, na * nj, recv_third, 0)
    lax.fori_loop(1, na * nk, recv_second, 0)

    depth = third_ref.shape[0]
    for s in range(na * nj):
        third_flat[s * depth:(s + 1) * depth, :] = third_all[s]
    width = second_ref.shape[0]
    for s in range(na * nk):
        second_flat[s * width:(s + 1) * width, :] = second_all[s]

    third = third_flat[...]
    second = second_flat[...]
    high, low = split(third)
    both = jnp.concatenate([high, low], axis=1)
    weights[...] = jnp.concatenate([both, both], axis=0)
    scale[...] = jnp.concatenate([second, second], axis=1)

    over_rows = (((0,), (0,)), ((), ()))
    gram3[ka] = lax.dot_general(
        third, third, over_rows, precision=HIGHEST, preferred_element_type=jnp.float32
    )
    gram2[ja] = lax.dot_general(
        second, second, over_rows, precision=HIGHEST, preferred_element_type=jnp.float32
    )

    def gram3_copy(d, at):
        return pltpu.make_async_remote_copy(
            src_ref=gram3.at[at], dst_ref=gram3.at[at],
            send_sem=gram3_send.at[d], recv_sem=gram3_recv.at[at],
            device_id=(ia, ja, lax.rem(ka + d, nk)), device_id_type=MESH,
        )

    def gram2_copy(d, at):
        return pltpu.make_async_remote_copy(
            src_ref=gram2.at[at], dst_ref=gram2.at[at],
            send_sem=gram2_send.at[d], recv_sem=gram2_recv.at[at],
            device_id=(ia, lax.rem(ja + d, nj), ka), device_id_type=MESH,
        )

    for d in range(1, nk):
        gram3_copy(d, ka).start()
    for d in range(1, nj):
        gram2_copy(d, ja).start()

    columns = x_hbm.shape[1]
    inner = x_hbm.shape[2]
    together = min(TOGETHER, chunk_rows)

    def chunk(c, carry):
        slot = lax.rem(c, buffers)
        x_copy(c).wait()
        base = lax.rem(c, per_owner) * chunk_rows

        def few(g, carry):
            i = g * together
            x = x_buf[slot, pl.ds(i, together)].reshape(together * columns, inner)
            high, low = split(x)
            y = jnp.dot(
                jnp.concatenate([high, low], axis=1), weights[...],
                preferred_element_type=jnp.float32,
            )
            y = y.reshape(together, columns // 8, 8, 2 * rank)
            y = y * scale[...].reshape(columns // 8, 8, 2 * rank)[None]
            part[pl.ds(base + i, together)] = jnp.sum(y, axis=1)
            return carry

        lax.fori_loop(0, chunk_rows // together, few, 0)

        @pl.when(c + buffers < chunks)
        def _():
            x_copy(c + buffers).start()

        return carry

    def term():
        both = jnp.sum(part[...], axis=1)
        return both[:, :rank] + both[:, rank:]

    def term_copy(turn):
        owner = owner_at(turn)
        return pltpu.make_async_remote_copy(
            src_ref=terms_out.at[turn], dst_ref=terms_in.at[own],
            send_sem=term_send.at[turn], recv_sem=term_recv.at[own],
            device_id=(ia, owner // nk, lax.rem(owner, nk)), device_id_type=MESH,
        )

    def for_other(turn, carry):
        lax.fori_loop(turn * per_owner, (turn + 1) * per_owner, chunk, 0)
        terms_out[turn] = term()
        term_copy(turn).start()
        return carry

    lax.fori_loop(0, n_owner - 1, for_other, 0)
    lax.fori_loop((n_owner - 1) * per_owner, n_owner * per_owner, chunk, 0)
    terms_in[own] = term()

    for d in range(1, nk):
        gram3_copy(d, lax.rem(ka + d, nk)).wait_recv()
    for d in range(1, nj):
        gram2_copy(d, lax.rem(ja + d, nj)).wait_recv()
    mixed = jnp.sum(gram2[...], axis=0) * jnp.sum(gram3[...], axis=0)
    gradient = jnp.dot(
        first_ref[...], mixed, precision=HIGHEST, preferred_element_type=jnp.float32
    )

    def recv_term(turn, carry):
        owner = owner_at(turn)
        pltpu.make_async_remote_copy(
            src_ref=terms_out.at[turn], dst_ref=terms_in.at[owner],
            send_sem=term_send.at[turn], recv_sem=term_recv.at[owner],
            device_id=(ia, owner // nk, lax.rem(owner, nk)), device_id_type=MESH,
        ).wait_recv()
        return carry

    lax.fori_loop(0, n_owner - 1, recv_term, 0)
    out_ref[...] = gradient - jnp.sum(terms_in[...], axis=0)

    def sent_third(d, carry):
        third_copy(d).wait_send()
        return carry

    def sent_second(d, carry):
        second_copy(d).wait_send()
        return carry

    def sent_term(turn, carry):
        term_copy(turn).wait_send()
        return carry

    lax.fori_loop(1, na * nj, sent_third, 0)
    lax.fori_loop(1, na * nk, sent_second, 0)
    for d in range(1, nk):
        gram3_copy(d, ka).wait_send()
    for d in range(1, nj):
        gram2_copy(d, ja).wait_send()
    lax.fori_loop(0, n_owner - 1, sent_term, 0)


def on_device(na, nj, nk, tensor, first, second, third):
    rows, rank = first.shape
    _, columns, inner = tensor.shape
    chunk_rows = min(CHUNK_ROWS, rows)
    buffers = min(BUFFERS, nj * nk * (rows // chunk_rows))
    dma = pltpu.SemaphoreType.DMA
    f32 = jnp.float32
    vmem = pl.BlockSpec(memory_space=pltpu.VMEM)
    return pl.pallas_call(
        functools.partial(kernel, na, nj, nk, chunk_rows, buffers),
        out_shape=jax.ShapeDtypeStruct((rows, rank), f32),
        in_specs=[pl.BlockSpec(memory_space=pl.ANY), vmem, vmem, vmem],
        out_specs=vmem,
        scratch_shapes=[
            pltpu.VMEM((buffers, chunk_rows, columns, inner), f32),
            dma((buffers,)),
            pltpu.VMEM((na * nj,) + third.shape, f32),
            dma((na * nj,)),
            dma((na * nj,)),
            pltpu.VMEM((na * nk,) + second.shape, f32),
            dma((na * nk,)),
            dma((na * nk,)),
            pltpu.VMEM((inner, rank), f32),
            pltpu.VMEM((columns, rank), f32),
            pltpu.VMEM((2 * inner, 2 * rank), jnp.bfloat16),
            pltpu.VMEM((columns, 2 * rank), f32),
            pltpu.VMEM((nk, rank, rank), f32),
            dma((nk,)),
            dma((nk,)),
            pltpu.VMEM((nj, rank, rank), f32),
            dma((nj,)),
            dma((nj,)),
            pltpu.VMEM((rows, 8, 2 * rank), f32),
            pltpu.VMEM((nj * nk, rows, rank), f32),
            pltpu.VMEM((nj * nk, rows, rank), f32),
            dma((nj * nk,)),
            dma((nj * nk,)),
        ],
        compiler_params=pltpu.CompilerParams(
            collective_id=0, has_side_effects=True, vmem_limit_bytes=56 * 2**20
        ),
        name="cp_gradient",
    )(tensor, first, second, third)


def solution(mesh):
    sizes = (mesh.shape["ia"], mesh.shape["ja"], mesh.shape["ka"])
    return jax.shard_map(
        functools.partial(on_device, *sizes),
        mesh=mesh,
        in_specs=(
            P("ia", "ja", "ka"),
            P(("ia", "ja", "ka"), None),
            P(("ja", "ia", "ka"), None),
            P(("ka", "ia", "ja"), None),
        ),
        out_specs=P(("ia", "ja", "ka"), None),
        check_vma=False,
    )
```

time: 202 us -> 59.8 us (0.30)
  blocking collectives: 93.4 us -> 0 us
  matrix products: 90.2 us -> 0 us
  Pallas kernels: 0 us -> 57.8 us
  between operations: 13.5 us -> 0.01 us
    dot_general x5 -> x0, matrix products: 90.2 us -> none  [the longest x1 74.8 us: on_device(): jnp.einsum('ijk,kr->ijr', tensor, third_block, precision=lax.Precision.HI...]
    pallas_call x0 -> x1, Pallas kernels: none -> 57.8 us  [on_device(): pl.pallas_call(functools.partial(kernel, na, nj, nk, chunk_rows, buffers)...]
    all_gather x2 -> x0, blocking collectives: 50.5 us -> none  [the longest x1 34.6 us: on_device(): third_block = lax.all_gather(factor_third, ('ia', 'ja'), axis=0, tiled=True)]
    psum x1 -> x0, blocking collectives: 42.9 us -> none  [on_device(): lax.psum((local_second, local_third), ('ia', 'ja', 'ka'))]
  transfers between devices with their start and end apart: 1 -> 0, of which waited for: 0 -> 0; matrix products, arithmetic and copies ran while one was open for 0% -> 0% of each run, Pallas kernels for 0% -> 0%
where the time goes in v1:
time: 59.8 us; the launch traced here: 59.1 us
  Pallas kernels  57.8 us (97%)
  local copies, waits for them, and re-layouts  1.32 us (2%)
    pallas_call x1, Pallas kernels, on_device(): pl.pallas_call(functools.partial(kernel, na, nj, nk, chunk_rows, buffers)...  57.8 us
    unnamed x1, local copies, waits for them, and re-layouts  1.32 us

profile of v1, /device:TPU:1, one launch (start us, length us, event | category | flops | bytes accessed | tf_op | source)
XLA Modules:
  0.0 59.1 jit_solution(7845541298325958698)
XLA Ops:
  0.0 57.8 %cp_gradient.1 = f32[32,32]{1,0:T(8,128)} custom-call(f32[256,256,256]{2,1,0:T(8,128)} %x_hbm.1, f32[32,32]{1,0:T(8,128)} %first_ref.1, f32[32,32]{1,0:T(8,128)} %second_ref.1, f32[16,32]{1,0:T(8,128)} %third_ref.1), custom_call_target="tpu_custom_call" | custom-call | tf_op jit(solution)/shard_map/cp_gradient/pallas_call | solution.py:286
  57.8 1.3 %copy.6 = f32[32,32]{1,0:T(8,128)} copy(f32[32,32]{1,0:T(8,128)} %cp_gradient.1) | data formatting | bytes 8192

commit v2 on v1

--- a/solution.py
+++ b/solution.py
@@ -9,7 +9,7 @@
 
 MESH = pl.DeviceIdType.MESH
 HIGHEST = lax.Precision.HIGHEST
-TOGETHER = 2
+TOGETHER = 8
 CHUNK_ROWS = 8
 BUFFERS = 20
 EARLY = 8

time: 59.8 us -> 41.9 us (0.70)
  Pallas kernels: 57.8 us -> 39.9 us
    pallas_call x1, Pallas kernels: 57.8 us -> 39.9 us  [on_device(): pl.pallas_call(functools.partial(kernel, na, nj, nk, chunk_rows, buffers)...]
where the time goes in v2:
time: 41.9 us; the launch traced here: 41.3 us
  Pallas kernels  39.9 us (95%)
  local copies, waits for them, and re-layouts  1.32 us (3%)
    pallas_call x1, Pallas kernels, on_device(): pl.pallas_call(functools.partial(kernel, na, nj, nk, chunk_rows, buffers)...  39.9 us
    unnamed x1, local copies, waits for them, and re-layouts  1.32 us

profile of v2, /device:TPU:1, one launch (start us, length us, event | category | flops | bytes accessed | tf_op | source)
XLA Modules:
  0.0 41.3 jit_solution(2143655992788998367)
XLA Ops:
  0.0 39.9 %cp_gradient.1 = f32[32,32]{1,0:T(8,128)} custom-call(f32[256,256,256]{2,1,0:T(8,128)} %x_hbm.1, f32[32,32]{1,0:T(8,128)} %first_ref.1, f32[32,32]{1,0:T(8,128)} %second_ref.1, f32[16,32]{1,0:T(8,128)} %third_ref.1), custom_call_target="tpu_custom_call" | custom-call | tf_op jit(solution)/shard_map/cp_gradient/pallas_call | solution.py:286
  39.9 1.3 %copy.6 = f32[32,32]{1,0:T(8,128)} copy(f32[32,32]{1,0:T(8,128)} %cp_gradient.1) | data formatting | bytes 8192

commit v3 on v2

--- a/solution.py
+++ b/solution.py
@@ -9,10 +9,10 @@
 
 MESH = pl.DeviceIdType.MESH
 HIGHEST = lax.Precision.HIGHEST
-TOGETHER = 8
-CHUNK_ROWS = 8
-BUFFERS = 20
-EARLY = 8
+PER_DOT = 4
+CHUNK_ROWS = 16
+BUFFERS = 10
+EARLY = 2
 
 
 def split(x):
@@ -54,9 +54,6 @@
         x_copy(c).start()
         return carry
 
-    early = min(EARLY, buffers)
-    lax.fori_loop(0, early, start_x, 0)
-
     def third_peer(d):
         at = lax.rem(ia * nj + ja + d, na * nj)
         return at // nj, lax.rem(at, nj)
@@ -82,6 +79,8 @@
             greet((lax.rem(ia + da, na), ja, pk))
         for dj in range(1, nj):
             greet((ia, lax.rem(ja + dj, nj), pk))
+    early = min(EARLY, buffers)
+    lax.fori_loop(0, early, start_x, 0)
     pl.semaphore_wait(barrier, na * nj - 1 + (nk - 1) * (na + nj - 1))
 
     third_at = ia * nj + ja
@@ -149,18 +148,20 @@
 
     third = third_flat[...]
     second = second_flat[...]
-    high, low = split(third)
-    both = jnp.concatenate([high, low], axis=1)
-    weights[...] = jnp.concatenate([both, both], axis=0)
+    both3 = jnp.concatenate(split(third), axis=1)
+    both2 = jnp.concatenate(split(second), axis=1)
+    weights[...] = jnp.concatenate([both3, both3], axis=0)
     scale[...] = jnp.concatenate([second, second], axis=1)
 
-    over_rows = (((0,), (0,)), ((), ()))
-    gram3[ka] = lax.dot_general(
-        third, third, over_rows, precision=HIGHEST, preferred_element_type=jnp.float32
-    )
-    gram2[ja] = lax.dot_general(
-        second, second, over_rows, precision=HIGHEST, preferred_element_type=jnp.float32
-    )
+    def gram_of(both):
+        pairs = lax.dot_general(
+            both, both, (((0,), (0,)), ((), ())), preferred_element_type=jnp.float32
+        )
+        halves = pairs[:rank] + pairs[rank:]
+        return halves[:, :rank] + halves[:, rank:]
+
+    gram3[ka] = gram_of(both3)
+    gram2[ja] = gram_of(both2)
 
     def gram3_copy(d, at):
         return pltpu.make_async_remote_copy(
@@ -183,27 +184,22 @@
 
     columns = x_hbm.shape[1]
     inner = x_hbm.shape[2]
-    together = min(TOGETHER, chunk_rows)
+    per = min(PER_DOT, chunk_rows)
 
     def chunk(c, carry):
         slot = lax.rem(c, buffers)
         x_copy(c).wait()
-        base = lax.rem(c, per_owner) * chunk_rows
-
-        def few(g, carry):
-            i = g * together
-            x = x_buf[slot, pl.ds(i, together)].reshape(together * columns, inner)
-            high, low = split(x)
+        sums = []
+        for i in range(0, chunk_rows, per):
+            x = x_buf[slot, i:i + per].reshape(per * columns, inner)
             y = jnp.dot(
-                jnp.concatenate([high, low], axis=1), weights[...],
+                jnp.concatenate(split(x), axis=1), weights[...],
                 preferred_element_type=jnp.float32,
             )
-            y = y.reshape(together, columns // 8, 8, 2 * rank)
-            y = y * scale[...].reshape(columns // 8, 8, 2 * rank)[None]
-            part[pl.ds(base + i, together)] = jnp.sum(y, axis=1)
-            return carry
-
-        lax.fori_loop(0, chunk_rows // together, few, 0)
+            y = y.reshape(per, columns, 2 * rank) * scale[...][None]
+            sums.append(jnp.sum(y, axis=1))
+        base = pl.multiple_of(lax.rem(c, per_owner) * chunk_rows, chunk_rows)
+        part[pl.ds(base, chunk_rows)] = jnp.concatenate(sums, axis=0)
 
         @pl.when(c + buffers < chunks)
         def _():
@@ -211,10 +207,6 @@
 
         return carry
 
-    def term():
-        both = jnp.sum(part[...], axis=1)
-        return both[:, :rank] + both[:, rank:]
-
     def term_copy(turn):
         owner = owner_at(turn)
         return pltpu.make_async_remote_copy(
@@ -223,15 +215,22 @@
             device_id=(ia, owner // nk, lax.rem(owner, nk)), device_id_type=MESH,
         )
 
-    def for_other(turn, carry):
+    def for_owner(turn, carry):
         lax.fori_loop(turn * per_owner, (turn + 1) * per_owner, chunk, 0)
-        terms_out[turn] = term()
-        term_copy(turn).start()
-        return carry
-
-    lax.fori_loop(0, n_owner - 1, for_other, 0)
-    lax.fori_loop((n_owner - 1) * per_owner, n_owner * per_owner, chunk, 0)
-    terms_in[own] = term()
+        term = part[:, :rank] + part[:, rank:]
+
+        @pl.when(turn < n_owner - 1)
+        def _():
+            terms_out[turn] = term
+            term_copy(turn).start()
+
+        @pl.when(turn == n_owner - 1)
+        def _():
+            terms_in[own] = term
+
+        return carry
+
+    lax.fori_loop(0, n_owner, for_owner, 0)
 
     for d in range(1, nk):
         gram3_copy(d, lax.rem(ka + d, nk)).wait_recv()
@@ -307,7 +306,7 @@
             pltpu.VMEM((nj, rank, rank), f32),
             dma((nj,)),
             dma((nj,)),
-            pltpu.VMEM((rows, 8, 2 * rank), f32),
+            pltpu.VMEM((rows, 2 * rank), f32),
             pltpu.VMEM((nj * nk, rows, rank), f32),
             pltpu.VMEM((nj * nk, rows, rank), f32),
             dma((nj * nk,)),

time: 41.9 us -> 38.3 us (0.914)
  Pallas kernels: 39.9 us -> 36.3 us
    pallas_call x1, Pallas kernels: 39.9 us -> 36.3 us  [on_device(): pl.pallas_call(functools.partial(kernel, na, nj, nk, chunk_rows, buffers)...]
where the time goes in v3:
time: 38.3 us; the launch traced here: 37.6 us
  Pallas kernels  36.3 us (95%)
  local copies, waits for them, and re-layouts  1.32 us (3%)
    pallas_call x1, Pallas kernels, on_device(): pl.pallas_call(functools.partial(kernel, na, nj, nk, chunk_rows, buffers)...  36.3 us
    unnamed x1, local copies, waits for them, and re-layouts  1.32 us

profile of v3, /device:TPU:1, one launch (start us, length us, event | category | flops | bytes accessed | tf_op | source)
XLA Modules:
  0.0 37.6 jit_solution(10672562843822533711)
XLA Ops:
  0.0 36.3 %cp_gradient.1 = f32[32,32]{1,0:T(8,128)} custom-call(f32[256,256,256]{2,1,0:T(8,128)} %x_hbm.1, f32[32,32]{1,0:T(8,128)} %first_ref.1, f32[32,32]{1,0:T(8,128)} %second_ref.1, f32[16,32]{1,0:T(8,128)} %third_ref.1), custom_call_target="tpu_custom_call" | custom-call | tf_op jit(solution)/shard_map/cp_gradient/pallas_call | solution.py:285
  36.3 1.3 %copy.6 = f32[32,32]{1,0:T(8,128)} copy(f32[32,32]{1,0:T(8,128)} %cp_gradient.1) | data formatting | bytes 8192

commit v4 on v3

--- a/solution.py
+++ b/solution.py
@@ -150,8 +150,9 @@
     second = second_flat[...]
     both3 = jnp.concatenate(split(third), axis=1)
     both2 = jnp.concatenate(split(second), axis=1)
-    weights[...] = jnp.concatenate([both3, both3], axis=0)
-    scale[...] = jnp.concatenate([second, second], axis=1)
+    turned = jnp.concatenate(split(second.T), axis=0)
+    weights[...] = jnp.concatenate([turned, turned], axis=1)
+    scale[...] = jnp.concatenate([third.T, third.T], axis=0)
 
     def gram_of(both):
         pairs = lax.dot_general(
@@ -189,17 +190,18 @@
     def chunk(c, carry):
         slot = lax.rem(c, buffers)
         x_copy(c).wait()
-        sums = []
-        for i in range(0, chunk_rows, per):
-            x = x_buf[slot, i:i + per].reshape(per * columns, inner)
-            y = jnp.dot(
-                jnp.concatenate(split(x), axis=1), weights[...],
+        base = pl.multiple_of(lax.rem(c, per_owner) * chunk_rows, chunk_rows)
+        found = []
+        for i in range(chunk_rows):
+            high, low = split(x_buf[slot, i])
+            z = jnp.dot(
+                weights[...], jnp.concatenate([high, low], axis=0),
                 preferred_element_type=jnp.float32,
             )
-            y = y.reshape(per, columns, 2 * rank) * scale[...][None]
-            sums.append(jnp.sum(y, axis=1))
-        base = pl.multiple_of(lax.rem(c, per_owner) * chunk_rows, chunk_rows)
-        part[pl.ds(base, chunk_rows)] = jnp.concatenate(sums, axis=0)
+            z = z * scale[...]
+            z = z[:rank] + z[rank:]
+            found.append(sum(z[:, at:at + 128] for at in range(0, inner, 128)))
+        part[pl.ds(base, chunk_rows)] = jnp.stack(found)
 
         @pl.when(c + buffers < chunks)
         def _():
@@ -217,7 +219,7 @@
 
     def for_owner(turn, carry):
         lax.fori_loop(turn * per_owner, (turn + 1) * per_owner, chunk, 0)
-        term = part[:, :rank] + part[:, rank:]
+        term = jnp.sum(part[...], axis=2)
 
         @pl.when(turn < n_owner - 1)
         def _():
@@ -298,15 +300,15 @@
             dma((na * nk,)),
             pltpu.VMEM((inner, rank), f32),
             pltpu.VMEM((columns, rank), f32),
-            pltpu.VMEM((2 * inner, 2 * rank), jnp.bfloat16),
-            pltpu.VMEM((columns, 2 * rank), f32),
+            pltpu.VMEM((2 * rank, 2 * columns), jnp.bfloat16),
+            pltpu.VMEM((2 * rank, inner), f32),
             pltpu.VMEM((nk, rank, rank), f32),
             dma((nk,)),
             dma((nk,)),
             pltpu.VMEM((nj, rank, rank), f32),
             dma((nj,)),
             dma((nj,)),
-            pltpu.VMEM((rows, 2 * rank), f32),
+            pltpu.VMEM((rows, rank, 128), f32),
             pltpu.VMEM((nj * nk, rows, rank), f32),
             pltpu.VMEM((nj * nk, rows, rank), f32),
             dma((nj * nk,)),

time: 38.3 us -> 34.2 us (0.89)
  the two profiles are of different devices: /device:TPU:1 before, /device:TPU:0 now
where the time goes in v4:
time: 34.2 us; the launch traced here: 33.8 us
  Pallas kernels  32.5 us (95%)
  local copies, waits for them, and re-layouts  1.32 us (4%)
    pallas_call x1, Pallas kernels, on_device(): pl.pallas_call(functools.partial(kernel, na, nj, nk, chunk_rows, buffers)...  32.5 us
    unnamed x1, local copies, waits for them, and re-layouts  1.32 us

profile of v4, /device:TPU:0, one launch (start us, length us, event | category | flops | bytes accessed | tf_op | source)
XLA Modules:
  0.0 33.8 jit_solution(3983639213699365173)
XLA Ops:
  0.0 32.5 %cp_gradient.1 = f32[32,32]{1,0:T(8,128)} custom-call(f32[256,256,256]{2,1,0:T(8,128)} %x_hbm.1, f32[32,32]{1,0:T(8,128)} %first_ref.1, f32[32,32]{1,0:T(8,128)} %second_ref.1, f32[16,32]{1,0:T(8,128)} %third_ref.1), custom_call_target="tpu_custom_call" | custom-call | tf_op jit(solution)/shard_map/cp_gradient/pallas_call | solution.py:287
  32.5 1.3 %copy.6 = f32[32,32]{1,0:T(8,128)} copy(f32[32,32]{1,0:T(8,128)} %cp_gradient.1) | data formatting | bytes 8192

commit v5 on v4

--- a/solution.py
+++ b/solution.py
@@ -9,10 +9,8 @@
 
 MESH = pl.DeviceIdType.MESH
 HIGHEST = lax.Precision.HIGHEST
-PER_DOT = 4
-CHUNK_ROWS = 16
-BUFFERS = 10
-EARLY = 2
+BUFFERS = 5
+EARLY = 1
 
 
 def split(x):
@@ -22,7 +20,7 @@
 
 
 def kernel(
-    na, nj, nk, chunk_rows, buffers,
+    na, nj, nk, buffers,
     x_hbm, first_ref, second_ref, third_ref, out_ref,
     x_buf, x_sem,
     third_all, third_send, third_recv,
@@ -30,24 +28,21 @@
     third_flat, second_flat, weights, scale,
     gram3, gram3_send, gram3_recv,
     gram2, gram2_send, gram2_recv,
-    part, terms_out, terms_in, term_send, term_recv,
+    terms_out, terms_in, term_send, term_recv,
 ):
     ia, ja, ka = lax.axis_index("ia"), lax.axis_index("ja"), lax.axis_index("ka")
     n_owner = nj * nk
     own = ja * nk + ka
     rows = out_ref.shape[0]
     rank = out_ref.shape[1]
-    per_owner = rows // chunk_rows
-    chunks = n_owner * per_owner
 
     def owner_at(turn):
         return lax.rem(own + 1 + turn, n_owner)
 
-    def x_copy(c):
-        start = owner_at(c // per_owner) * rows + lax.rem(c, per_owner) * chunk_rows
-        slot = lax.rem(c, buffers)
+    def x_copy(turn):
+        slot = lax.rem(turn, buffers)
         return pltpu.make_async_copy(
-            x_hbm.at[pl.ds(start, chunk_rows)], x_buf.at[slot], x_sem.at[slot]
+            x_hbm.at[pl.ds(owner_at(turn) * rows, rows)], x_buf.at[slot], x_sem.at[slot]
         )
 
     def start_x(c, carry):
@@ -110,8 +105,8 @@
         second_copy(d).start()
         return carry
 
+    lax.fori_loop(1, na * nk, start_second, 0)
     lax.fori_loop(1, na * nj, start_third, 0)
-    lax.fori_loop(1, na * nk, start_second, 0)
     lax.fori_loop(early, buffers, start_x, 0)
     third_all[third_at] = third_ref[...]
     second_all[second_at] = second_ref[...]
@@ -136,90 +131,74 @@
         ).wait_recv()
         return carry
 
+    def gram3_copy(d, at):
+        return pltpu.make_async_remote_copy(
+            src_ref=gram3.at[at], dst_ref=gram3.at[at],
+            send_sem=gram3_send.at[d], recv_sem=gram3_recv.at[at],
+            device_id=(ia, ja, lax.rem(ka + d, nk)), device_id_type=MESH,
+        )
+
+    def gram2_copy(d, at):
+        return pltpu.make_async_remote_copy(
+            src_ref=gram2.at[at], dst_ref=gram2.at[at],
+            send_sem=gram2_send.at[d], recv_sem=gram2_recv.at[at],
+            device_id=(ia, lax.rem(ja + d, nj), ka), device_id_type=MESH,
+        )
+
+    def gram_of(turned):
+        pairs = lax.dot_general(
+            turned, turned, (((1,), (1,)), ((), ())), preferred_element_type=jnp.float32
+        )
+        halves = pairs[:rank] + pairs[rank:]
+        return halves[:, :rank] + halves[:, rank:]
+
+    lax.fori_loop(1, na * nk, recv_second, 0)
+    width = second_ref.shape[0]
+    for s in range(na * nk):
+        second_flat[s * width:(s + 1) * width, :] = second_all[s]
+    turned2 = jnp.concatenate(split(second_flat[...].T), axis=0)
+    weights[...] = jnp.concatenate([turned2, turned2], axis=1)
+    gram2[ja] = gram_of(turned2)
+    for d in range(1, nj):
+        gram2_copy(d, ja).start()
+
     lax.fori_loop(1, na * nj, recv_third, 0)
-    lax.fori_loop(1, na * nk, recv_second, 0)
-
     depth = third_ref.shape[0]
     for s in range(na * nj):
         third_flat[s * depth:(s + 1) * depth, :] = third_all[s]
-    width = second_ref.shape[0]
-    for s in range(na * nk):
-        second_flat[s * width:(s + 1) * width, :] = second_all[s]
-
-    third = third_flat[...]
-    second = second_flat[...]
-    both3 = jnp.concatenate(split(third), axis=1)
-    both2 = jnp.concatenate(split(second), axis=1)
-    turned = jnp.concatenate(split(second.T), axis=0)
-    weights[...] = jnp.concatenate([turned, turned], axis=1)
-    scale[...] = jnp.concatenate([third.T, third.T], axis=0)
-
-    def gram_of(both):
-        pairs = lax.dot_general(
-            both, both, (((0,), (0,)), ((), ())), preferred_element_type=jnp.float32
-        )
-        halves = pairs[:rank] + pairs[rank:]
-        return halves[:, :rank] + halves[:, rank:]
-
-    gram3[ka] = gram_of(both3)
-    gram2[ja] = gram_of(both2)
-
-    def gram3_copy(d, at):
-        return pltpu.make_async_remote_copy(
-            src_ref=gram3.at[at], dst_ref=gram3.at[at],
-            send_sem=gram3_send.at[d], recv_sem=gram3_recv.at[at],
-            device_id=(ia, ja, lax.rem(ka + d, nk)), device_id_type=MESH,
-        )
-
-    def gram2_copy(d, at):
-        return pltpu.make_async_remote_copy(
-            src_ref=gram2.at[at], dst_ref=gram2.at[at],
-            send_sem=gram2_send.at[d], recv_sem=gram2_recv.at[at],
-            device_id=(ia, lax.rem(ja + d, nj), ka), device_id_type=MESH,
-        )
-
+    third = third_flat[...].T
+    scale[...] = jnp.concatenate([third, third], axis=0)
+    gram3[ka] = gram_of(jnp.concatenate(split(third), axis=0))
     for d in range(1, nk):
         gram3_copy(d, ka).start()
-    for d in range(1, nj):
-        gram2_copy(d, ja).start()
-
-    columns = x_hbm.shape[1]
+
     inner = x_hbm.shape[2]
-    per = min(PER_DOT, chunk_rows)
-
-    def chunk(c, carry):
-        slot = lax.rem(c, buffers)
-        x_copy(c).wait()
-        base = pl.multiple_of(lax.rem(c, per_owner) * chunk_rows, chunk_rows)
+
+    def term_copy(turn):
+        owner = owner_at(turn)
+        return pltpu.make_async_remote_copy(
+            src_ref=terms_out.at[turn], dst_ref=terms_in.at[own],
+            send_sem=term_send.at[turn], recv_sem=term_recv.at[own],
+            device_id=(ia, owner // nk, lax.rem(owner, nk)), device_id_type=MESH,
+        )
+
+    def for_owner(turn, carry):
+        slot = lax.rem(turn, buffers)
+        x_copy(turn).wait()
         found = []
-        for i in range(chunk_rows):
-            high, low = split(x_buf[slot, i])
+        for i in range(rows):
             z = jnp.dot(
-                weights[...], jnp.concatenate([high, low], axis=0),
+                weights[...], jnp.concatenate(split(x_buf[slot, i]), axis=0),
                 preferred_element_type=jnp.float32,
             )
             z = z * scale[...]
             z = z[:rank] + z[rank:]
             found.append(sum(z[:, at:at + 128] for at in range(0, inner, 128)))
-        part[pl.ds(base, chunk_rows)] = jnp.stack(found)
-
-        @pl.when(c + buffers < chunks)
+        term = jnp.sum(jnp.stack(found), axis=2)
+
+        @pl.when(turn + buffers < n_owner)
         def _():
-            x_copy(c + buffers).start()
-
-        return carry
-
-    def term_copy(turn):
-        owner = owner_at(turn)
-        return pltpu.make_async_remote_copy(
-            src_ref=terms_out.at[turn], dst_ref=terms_in.at[own],
-            send_sem=term_send.at[turn], recv_sem=term_recv.at[own],
-            device_id=(ia, owner // nk, lax.rem(owner, nk)), device_id_type=MESH,
-        )
-
-    def for_owner(turn, carry):
-        lax.fori_loop(turn * per_owner, (turn + 1) * per_owner, chunk, 0)
-        term = jnp.sum(part[...], axis=2)
+            x_copy(turn + buffers).start()
 
         @pl.when(turn < n_owner - 1)
         def _():
@@ -253,7 +232,7 @@
         return carry
 
     lax.fori_loop(0, n_owner - 1, recv_term, 0)
-    out_ref[...] = gradient - jnp.sum(terms_in[...], axis=0)
+    out_ref[...] = jnp.sum(terms_in[...], axis=0) - gradient
 
     def sent_third(d, carry):
         third_copy(d).wait_send()
@@ -279,18 +258,17 @@
 def on_device(na, nj, nk, tensor, first, second, third):
     rows, rank = first.shape
     _, columns, inner = tensor.shape
-    chunk_rows = min(CHUNK_ROWS, rows)
-    buffers = min(BUFFERS, nj * nk * (rows // chunk_rows))
+    buffers = min(BUFFERS, nj * nk)
     dma = pltpu.SemaphoreType.DMA
     f32 = jnp.float32
     vmem = pl.BlockSpec(memory_space=pltpu.VMEM)
-    return pl.pallas_call(
-        functools.partial(kernel, na, nj, nk, chunk_rows, buffers),
+    return -pl.pallas_call(
+        functools.partial(kernel, na, nj, nk, buffers),
         out_shape=jax.ShapeDtypeStruct((rows, rank), f32),
         in_specs=[pl.BlockSpec(memory_space=pl.ANY), vmem, vmem, vmem],
         out_specs=vmem,
         scratch_shapes=[
-            pltpu.VMEM((buffers, chunk_rows, columns, inner), f32),
+            pltpu.VMEM((buffers, rows, columns, inner), f32),
             dma((buffers,)),
             pltpu.VMEM((na * nj,) + third.shape, f32),
             dma((na * nj,)),
@@ -308,14 +286,13 @@
             pltpu.VMEM((nj, rank, rank), f32),
             dma((nj,)),
             dma((nj,)),
-            pltpu.VMEM((rows, rank, 128), f32),
             pltpu.VMEM((nj * nk, rows, rank), f32),
             pltpu.VMEM((nj * nk, rows, rank), f32),
             dma((nj * nk,)),
             dma((nj * nk,)),
         ],
         compiler_params=pltpu.CompilerParams(
-            collective_id=0, has_side_effects=True, vmem_limit_bytes=56 * 2**20
+            collective_id=0, has_side_effects=True, vmem_limit_bytes=48 * 2**20
         ),
         name="cp_gradient",
     )(tensor, first, second, third)

time: 34.2 us -> 32.6 us (0.953)
  the two profiles are of different devices: /device:TPU:0 before, /device:TPU:1 now
where the time goes in v5:
time: 32.6 us; the launch traced here: 32.2 us
  Pallas kernels  29.4 us (90%)
  local copies, waits for them, and re-layouts  2.13 us (7%)
  other arithmetic  0.61 us (2%)
    pallas_call x1, Pallas kernels, on_device(): pl.pallas_call(functools.partial(kernel, na, nj, nk, buffers), out_shape=...  29.4 us
    unnamed x6, local copies, waits for them, and re-layouts  2.13 us

profile of v5, /device:TPU:1, one launch (start us, length us, event | category | flops | bytes accessed | tf_op | source)
XLA Modules:
  0.0 32.2 jit_solution(14825304213870428444)
XLA Ops:
  0.0 0.0 copy-start
  0.0 0.7 %copy-done = f32[32,32]{1,0:T(8,128)S(1)} copy-done((f32[32,32]{1,0:T(8,128)S(1)}, f32[32,32]{1,0:T(8,128)}, u32[]{:S(2)}) %copy-start) | copy-done | bytes 4120
  0.7 0.0 copy-start.1
  0.7 0.7 %copy-done.1 = f32[32,32]{1,0:T(8,128)S(1)} copy-done((f32[32,32]{1,0:T(8,128)S(1)}, f32[32,32]{1,0:T(8,128)}, u32[]{:S(2)}) %copy-start.1) | copy-done | bytes 4120
  1.4 0.0 copy-start.2
  1.4 0.7 %copy-done.2 = f32[16,32]{1,0:T(8,128)S(1)} copy-done((f32[16,32]{1,0:T(8,128)S(1)}, f32[16,32]{1,0:T(8,128)}, u32[]{:S(2)}) %copy-start.2) | copy-done | bytes 2072
  2.1 29.4 %cp_gradient.1 = f32[32,32]{1,0:T(8,128)S(1)} custom-call(f32[256,256,256]{2,1,0:T(8,128)} %x_hbm.1, f32[32,32]{1,0:T(8,128)S(1)} %copy-done, f32[32,32]{1,0:T(8,128)S(1)} %copy-done.1, f32[16,32]{1,0:T(8,128)S(1)} %copy-done.2), custom_call_target="tpu_custom_call" | custom-call | tf_op jit(solution)/shard_map/cp_gradient/pallas_call | solution.py:265
  31.6 0.6 %neg.3 = f32[32,32]{1,0:T(8,128)} negate(f32[32,32]{1,0:T(8,128)S(1)} %cp_gradient.1) | non-fusion elementwise | flops 1024 | bytes 8192 | tf_op jit(solution)/shard_map/neg | solution.py:265
Async XLA Ops:
  0.0 0.7 %copy-start = (f32[32,32]{1,0:T(8,128)S(1)}, f32[32,32]{1,0:T(8,128)}, u32[]{:S(2)}) copy-start(f32[32,32]{1,0:T(8,128)} %first_ref.1) | copy-start | bytes 12292
  0.7 0.7 %copy-start.1 = (f32[32,32]{1,0:T(8,128)S(1)}, f32[32,32]{1,0:T(8,128)}, u32[]{:S(2)}) copy-start(f32[32,32]{1,0:T(8,128)} %second_ref.1) | copy-start | bytes 12292
  1.4 0.7 %copy-start.2 = (f32[16,32]{1,0:T(8,128)S(1)}, f32[16,32]{1,0:T(8,128)}, u32[]{:S(2)}) copy-start(f32[16,32]{1,0:T(8,128)} %third_ref.1) | copy-start | bytes 6148

commit v6 on v5

--- a/solution.py
+++ b/solution.py
@@ -21,7 +21,8 @@
 
 def kernel(
     na, nj, nk, buffers,
-    x_hbm, first_ref, second_ref, third_ref, out_ref,
+    x_hbm, first_hbm, second_hbm, third_hbm, out_ref,
+    first_ref, near_sem,
     x_buf, x_sem,
     third_all, third_send, third_recv,
     second_all, second_send, second_recv,
@@ -49,6 +50,18 @@
         x_copy(c).start()
         return carry
 
+    third_at = ia * nj + ja
+    second_at = ia * nk + ka
+    third_ref, second_ref = third_all.at[third_at], second_all.at[second_at]
+    near = [
+        pltpu.make_async_copy(source, target, near_sem.at[k])
+        for k, (source, target) in enumerate(
+            [(second_hbm, second_ref), (third_hbm, third_ref), (first_hbm, first_ref)]
+        )
+    ]
+    for copy in near:
+        copy.start()
+
     def third_peer(d):
         at = lax.rem(ia * nj + ja + d, na * nj)
         return at // nj, lax.rem(at, nj)
@@ -78,9 +91,6 @@
     lax.fori_loop(0, early, start_x, 0)
     pl.semaphore_wait(barrier, na * nj - 1 + (nk - 1) * (na + nj - 1))
 
-    third_at = ia * nj + ja
-    second_at = ia * nk + ka
-
     def third_copy(d):
         pa, pj = third_peer(d)
         return pltpu.make_async_remote_copy(
@@ -105,11 +115,11 @@
         second_copy(d).start()
         return carry
 
+    near[0].wait()
     lax.fori_loop(1, na * nk, start_second, 0)
+    near[1].wait()
     lax.fori_loop(1, na * nj, start_third, 0)
     lax.fori_loop(early, buffers, start_x, 0)
-    third_all[third_at] = third_ref[...]
-    second_all[second_at] = second_ref[...]
 
     def recv_third(d, carry):
         pa, pj = third_peer(d)
@@ -153,7 +163,7 @@
         return halves[:, :rank] + halves[:, rank:]
 
     lax.fori_loop(1, na * nk, recv_second, 0)
-    width = second_ref.shape[0]
+    width = second_hbm.shape[0]
     for s in range(na * nk):
         second_flat[s * width:(s + 1) * width, :] = second_all[s]
     turned2 = jnp.concatenate(split(second_flat[...].T), axis=0)
@@ -163,7 +173,7 @@
         gram2_copy(d, ja).start()
 
     lax.fori_loop(1, na * nj, recv_third, 0)
-    depth = third_ref.shape[0]
+    depth = third_hbm.shape[0]
     for s in range(na * nj):
         third_flat[s * depth:(s + 1) * depth, :] = third_all[s]
     third = third_flat[...].T
@@ -184,6 +194,19 @@
 
     def for_owner(turn, carry):
         slot = lax.rem(turn, buffers)
+
+        @pl.when(turn == n_owner - 1)
+        def _():
+            near[2].wait()
+            for d in range(1, nk):
+                gram3_copy(d, lax.rem(ka + d, nk)).wait_recv()
+            for d in range(1, nj):
+                gram2_copy(d, lax.rem(ja + d, nj)).wait_recv()
+            mixed = jnp.sum(gram2[...], axis=0) * jnp.sum(gram3[...], axis=0)
+            out_ref[...] = -jnp.dot(
+                first_ref[...], mixed, precision=HIGHEST, preferred_element_type=jnp.float32
+            )
+
         x_copy(turn).wait()
         found = []
         for i in range(rows):
@@ -213,15 +236,6 @@
 
     lax.fori_loop(0, n_owner, for_owner, 0)
 
-    for d in range(1, nk):
-        gram3_copy(d, lax.rem(ka + d, nk)).wait_recv()
-    for d in range(1, nj):
-        gram2_copy(d, lax.rem(ja + d, nj)).wait_recv()
-    mixed = jnp.sum(gram2[...], axis=0) * jnp.sum(gram3[...], axis=0)
-    gradient = jnp.dot(
-        first_ref[...], mixed, precision=HIGHEST, preferred_element_type=jnp.float32
-    )
-
     def recv_term(turn, carry):
         owner = owner_at(turn)
         pltpu.make_async_remote_copy(
@@ -232,7 +246,7 @@
         return carry
 
     lax.fori_loop(0, n_owner - 1, recv_term, 0)
-    out_ref[...] = jnp.sum(terms_in[...], axis=0) - gradient
+    out_ref[...] += jnp.sum(terms_in[...], axis=0)
 
     def sent_third(d, carry):
         third_copy(d).wait_send()
@@ -264,10 +278,12 @@
     vmem = pl.BlockSpec(memory_space=pltpu.VMEM)
     return -pl.pallas_call(
         functools.partial(kernel, na, nj, nk, buffers),
-        out_shape=jax.ShapeDtypeStruct((rows, rank), f32),
-        in_specs=[pl.BlockSpec(memory_space=pl.ANY), vmem, vmem, vmem],
+        out_shape=pltpu.VMEM((rows, rank), f32),
+        in_specs=[pl.BlockSpec(memory_space=pltpu.HBM)] * 4,
         out_specs=vmem,
         scratch_shapes=[
+            pltpu.VMEM(first.shape, f32),
+            dma((3,)),
             pltpu.VMEM((buffers, rows, columns, inner), f32),
             dma((buffers,)),
             pltpu.VMEM((na * nj,) + third.shape, f32),
@@ -292,7 +308,7 @@
             dma((nj * nk,)),
         ],
         compiler_params=pltpu.CompilerParams(
-            collective_id=0, has_side_effects=True, vmem_limit_bytes=48 * 2**20
+            collective_id=0, has_side_effects=True, vmem_limit_bytes=56 * 2**20
         ),
         name="cp_gradient",
     )(tensor, first, second, third)

time: 32.6 us -> 30.3 us (0.929)
  local copies, waits for them, and re-layouts: 2.13 us -> 0 us
    unnamed x6 -> x0, local copies, waits for them, and re-layouts: 2.13 us -> none
where the time goes in v6:
time: 30.3 us; the launch traced here: 30.1 us
  Pallas kernels  29.5 us (97%)
  other arithmetic  0.61 us (2%)
    pallas_call x1, Pallas kernels, on_device(): pl.pallas_call(functools.partial(kernel, na, nj, nk, buffers), out_shape=...  29.5 us
    neg x1, other arithmetic, on_device(): -pl.pallas_call(functools.partial(kernel, na, nj, nk, buffers), out_shape...  0.61 us

profile of v6, /device:TPU:1, one launch (start us, length us, event | category | flops | bytes accessed | tf_op | source)
XLA Modules:
  0.0 30.1 jit_solution(11747872792663193901)
XLA Ops:
  0.0 29.5 %cp_gradient.1 = f32[32,32]{1,0:T(8,128)S(1)} custom-call(f32[256,256,256]{2,1,0:T(8,128)} %x_hbm.1, f32[32,32]{1,0:T(8,128)} %first_hbm.1, f32[32,32]{1,0:T(8,128)} %second_hbm.1, f32[16,32]{1,0:T(8,128)} %third_hbm.1), custom_call_target="tpu_custom_call" | custom-call | tf_op jit(solution)/shard_map/cp_gradient/pallas_call | solution.py:279
  29.5 0.6 %neg.3 = f32[32,32]{1,0:T(8,128)} negate(f32[32,32]{1,0:T(8,128)S(1)} %cp_gradient.1) | non-fusion elementwise | flops 1024 | bytes 8192 | tf_op jit(solution)/shard_map/neg | solution.py:279

commit v7 on v6

--- a/solution.py
+++ b/solution.py
@@ -10,7 +10,7 @@
 MESH = pl.DeviceIdType.MESH
 HIGHEST = lax.Precision.HIGHEST
 BUFFERS = 5
-EARLY = 1
+EARLY = 2
 
 
 def split(x):
@@ -177,7 +177,7 @@
     for s in range(na * nj):
         third_flat[s * depth:(s + 1) * depth, :] = third_all[s]
     third = third_flat[...].T
-    scale[...] = jnp.concatenate([third, third], axis=0)
+    scale[...] = third
     gram3[ka] = gram_of(jnp.concatenate(split(third), axis=0))
     for d in range(1, nk):
         gram3_copy(d, ka).start()
@@ -214,8 +214,7 @@
                 weights[...], jnp.concatenate(split(x_buf[slot, i]), axis=0),
                 preferred_element_type=jnp.float32,
             )
-            z = z * scale[...]
-            z = z[:rank] + z[rank:]
+            z = (z[:rank] + z[rank:]) * scale[...]
             found.append(sum(z[:, at:at + 128] for at in range(0, inner, 128)))
         term = jnp.sum(jnp.stack(found), axis=2)
 
@@ -295,7 +294,7 @@
             pltpu.VMEM((inner, rank), f32),
             pltpu.VMEM((columns, rank), f32),
             pltpu.VMEM((2 * rank, 2 * columns), jnp.bfloat16),
-            pltpu.VMEM((2 * rank, inner), f32),
+            pltpu.VMEM((rank, inner), f32),
             pltpu.VMEM((nk, rank, rank), f32),
             dma((nk,)),
             dma((nk,)),

time: 30.3 us -> 29.6 us (0.977)
  Pallas kernels: 29.5 us -> 28.8 us
    pallas_call x1, Pallas kernels: 29.5 us -> 28.8 us  [on_device(): pl.pallas_call(functools.partial(kernel, na, nj, nk, buffers), out_shape=...]
where the time goes in v7:
time: 29.6 us; the launch traced here: 29.4 us
  Pallas kernels  28.8 us (97%)
  other arithmetic  0.61 us (2%)
    pallas_call x1, Pallas kernels, on_device(): pl.pallas_call(functools.partial(kernel, na, nj, nk, buffers), out_shape=...  28.8 us
    neg x1, other arithmetic, on_device(): -pl.pallas_call(functools.partial(kernel, na, nj, nk, buffers), out_shape...  0.61 us

profile of v7, /device:TPU:1, one launch (start us, length us, event | category | flops | bytes accessed | tf_op | source)
XLA Modules:
  0.0 29.4 jit_solution(12619240348371795379)
XLA Ops:
  0.0 28.8 %cp_gradient.1 = f32[32,32]{1,0:T(8,128)S(1)} custom-call(f32[256,256,256]{2,1,0:T(8,128)} %x_hbm.1, f32[32,32]{1,0:T(8,128)} %first_hbm.1, f32[32,32]{1,0:T(8,128)} %second_hbm.1, f32[16,32]{1,0:T(8,128)} %third_hbm.1), custom_call_target="tpu_custom_call" | custom-call | tf_op jit(solution)/shard_map/cp_gradient/pallas_call | solution.py:278
  28.8 0.6 %neg.3 = f32[32,32]{1,0:T(8,128)} negate(f32[32,32]{1,0:T(8,128)S(1)} %cp_gradient.1) | non-fusion elementwise | flops 1024 | bytes 8192 | tf_op jit(solution)/shard_map/neg | solution.py:278
